TPU v7x, 512 devices: a whole 4x4x16 slice. The times are simulated.
512 devices in a mesh: row: 32 (over z_lo, y), col: 16 (over x, z_hi, core).
Axes of the slice: x: 4, y: 4, z: 16 (z_hi: 2, z_lo: 8; z = z_hi * 8 + z_lo), core: 2. Of those that a mesh axis runs over, the one named last changes fastest.
Arguments:
- covariance: float32 [12288, 12288], P('row', 'col'), as said below
- rotations: float32 [2, 16, 768, 768], P(None, 'col', 'row')
- flips: int32 [2, 16], replicated, may hold values 0 or 1
Outputs:
- rotated: float32 [12288, 12288], P('row', 'col')
Inputs may be any that keep to these rules, and one draw needn't show every extreme that they name: covariance is exactly symmetric.
All inputs are finite; a program needn't handle non-finite values.
Results may differ from a plain program's by a relative error of at most 0.00019.
Values sent between devices are 32-bit elements; how exact they have to be, the bound alone decides.
A program may use at most 64 MiB of HBM per device.

v0:
```python
import jax
import jax.numpy as jnp
import numpy as np
from jax import lax
from jax.sharding import PartitionSpec as P

ROUNDS = 2


def broadcast(value, axis, source):
    kept = jnp.where(lax.axis_index(axis) == source, value, 0).astype(value.dtype)
    return lax.psum(kept, axis)


def partner_2(value, axis, bit):
    return lax.ppermute(value, axis, [(i, i ^ 1 << bit) for i in range(lax.axis_size(axis))])


def from_behind(block, axis, distance):
    devices = range(lax.axis_size(axis))
    route = [(i - distance, i) for i in devices if i - distance in devices]
    return lax.ppermute(block, axis, route)


def trade_halves(block, half_width):
    return jnp.concatenate([block[:, half_width:], block[:, :half_width]], 1)


def contract_rows(first, second):
    return lax.dot_general(
        first,
        second,
        (((0,), (0,)), ((), ())),
        precision=lax.Precision.HIGHEST,
        preferred_element_type=jnp.float32,
    )


def source_table(row_count):
    pair_total = row_count // 2
    table = []
    for place in range(row_count):
        pair_of = place // 2
        if place % 2 == 0:
            table.append(0 if pair_of == 0 else 1 if pair_of == 1 else 2 * (pair_of - 1))
        else:
            table.append(
                2 * (pair_of + 1) + 1 if pair_of < pair_total - 1 else 2 * (pair_total - 1)
            )
    return np.array(table, dtype=np.int32)


def per_device(covariance, rotations, flips):
    tile = covariance
    block_rows = tile.shape[0]
    row_index = lax.axis_index("row")
    col_index = lax.axis_index("col")
    col_count = lax.axis_size("col")
    row_count = lax.axis_size("row")
    parity = row_index % 2
    home = row_index // 2
    for step in range(ROUNDS):
        shard = rotations[step, 0]
        whole = lax.all_gather(shard, "row", axis=0, tiled=True)
        own_flip = flips[step][col_index]
        home_flip = flips[step][home]
        right = jnp.dot(
            tile, whole, precision=lax.Precision.HIGHEST, preferred_element_type=jnp.float32
        )
        piece = lax.dynamic_slice_in_dim(whole, parity * block_rows, block_rows, 1)
        piece = broadcast(piece, "col", home)
        partner = partner_2(right, "row", 0)
        stacked = jnp.where(
            parity == 0, jnp.concatenate([right, partner], 0), jnp.concatenate([partner, right], 0)
        )
        fresh = contract_rows(piece, stacked)
        mirror = partner_2(fresh, "row", 0)
        fresh = jnp.where(home_flip == 1, mirror, fresh)
        fresh = jnp.where(own_flip == 1, trade_halves(fresh, block_rows), fresh)
        if step + 1 < ROUNDS:
            upper = fresh[:, :block_rows]
            lower = fresh[:, block_rows:]
            outgoing = jnp.where(col_index == 0, lower, upper)
            from_left = from_behind(outgoing, "col", 1)
            from_right = from_behind(lower, "col", -1)
            new_upper = jnp.where(col_index == 0, upper, from_left)
            new_lower = jnp.where(col_index == col_count - 1, upper, from_right)
            fresh = jnp.concatenate([new_upper, new_lower], 1)
            width = fresh.shape[1] // row_count
            sliced = fresh.reshape(block_rows, row_count, width)
            spread = lax.all_to_all(sliced, "row", split_axis=1, concat_axis=1, tiled=True)
            ordered = spread[:, source_table(row_count), :]
            collected = lax.all_to_all(ordered, "row", split_axis=1, concat_axis=1, tiled=True)
            fresh = collected.reshape(block_rows, row_count * width)
        tile = fresh
    return tile


def solution(mesh):
    placed = (P("row", "col"), P(None, "col", "row", None), P())
    return jax.shard_map(
        per_device, mesh=mesh, in_specs=placed, out_specs=P("row", "col"), check_vma=False
    )
```

profile of v0, /device:TPU:2, one launch (start us, length us, event | category | flops | bytes accessed | tf_op | source)
XLA Modules:
  0.0 1097.0 jit_solution(3108691062499740948)
XLA Ops:
  6.5 0.0 copy-start
  6.5 0.0 all-gather.7.cloned.1.call-start
  6.5 1.7 fusion.22
  8.2 0.0 all-gather.7.cloned.1.call-update
  8.2 0.0 all-gather.5.cloned.1.call-start
  8.3 0.7 all-gather.5.cloned.1.call-update
  9.0 0.0 all-reduce.3.cloned.1.call-start
  9.1 229.7 %all-gather.7.cloned.1.call-done = f32[1,1,768,768]{3,2,1,0:T(8,128)} async-done(((f32[1,1,24,768]{3,2,1,0:T(8,128)}), f32[1,1,768,768]{3,2,1,0:T(8,128)}) %all-gather.7.cloned.1.call-update) | async-done | bytes 2359312 | tf_op jit(solution)/shard_map/all_gather | solution.py:64
  238.8 2.4 select_bitcast_fusion
  241.2 222.7 %all-gather.5.cloned.1.call-done = f32[1,1,768,768]{3,2,1,0:T(8,128)} async-done(((f32[1,1,24,768]{3,2,1,0:T(8,128)}), f32[1,1,768,768]{3,2,1,0:T(8,128)}) %all-gather.5.cloned.1.call-update) | async-done | bytes 2359312 | tf_op jit(solution)/shard_map/all_gather | solution.py:64
  463.8 2.4 select_bitcast_fusion.1
  466.2 0.0 all-reduce.3.cloned.1.call-update
  466.2 1.6 copy-done.2
  467.9 4.1 fusion.14
  471.9 3.5 collective-permute-start
  475.5 14.7 %collective-permute-done = f32[384,768]{1,0:T(8,128)S(1)} collective-permute-done((f32[384,768]{1,0:T(8,128)}, f32[384,768]{1,0:T(8,128)S(1)}, u32[]{:S(2)}, u32[]{:S(2)}) %collective-permute-start) | collective-permute-done | bytes 1179680 | tf_op jit(solution)/shard_map/ppermute | solution.py:16
  490.2 299.4 %all-reduce.3.cloned.1.call-done = (f32[768,384]{1,0:T(8,128)}, f32[768,384]{1,0:T(8,128)}) async-done(((f32[768,384]{1,0:T(8,128)}, f32[768,384]{1,0:T(8,128)}), (f32[768,384]{1,0:T(8,128)}, f32[768,384]{1,0:T(8,128)})) %all-reduce.3.cloned.1.call-update) | async-done | bytes 2359312 | tf_op jit(solution)/shard_map/psum | solution.py:12
  789.7 5.1 fusion
  794.8 10.6 collective-permute-start.1
  805.4 0.0 copy-done.3
  805.4 0.7 constant_dynamic-slice_fusion.1
  807.4 24.3 %collective-permute-done.1 = f32[384,768]{1,0:T(8,128)S(1)} collective-permute-done((f32[384,768]{1,0:T(8,128)S(1)}, f32[384,768]{1,0:T(8,128)S(1)}, u32[]{:S(2)}, u32[]{:S(2)}) %collective-permute-start.1) | collective-permute-done | bytes 1179680 | tf_op jit(solution)/shard_map/ppermute | solution.py:16
  831.7 0.1 broadcast_select_fusion
  831.9 0.1 fusion.21
  831.9 0.1 maximum_select_fusion.4
  832.1 0.1 slice_select_fusion.2
  832.2 1.9 collective-permute-start.2
  834.1 13.3 %collective-permute-start.3 = (f32[384,384]{1,0:T(8,128)S(1)}, f32[384,384]{1,0:T(8,128)}, u32[]{:S(2)}, u32[]{:S(2)}) collective-permute-start(f32[384,384]{1,0:T(8,128)S(1)} %get-tuple-element.12), channel_id=1, source_target_pairs={{1,0},{2,1},{3,2},{4,3},{5,4},{6,5},{7,6},{8,7},{9,8},{10,9},{11,1... | collective-permute-start | bytes 1769480 | tf_op jit(solution)/shard_map/ppermute | solution.py:22
  847.4 27.1 %collective-permute-done.2 = f32[384,384]{1,0:T(8,128)} collective-permute-done((f32[384,384]{1,0:T(8,128)S(1)}, f32[384,384]{1,0:T(8,128)}, u32[]{:S(2)}, u32[]{:S(2)}) %collective-permute-start.2) | collective-permute-done | bytes 589856 | tf_op jit(solution)/shard_map/ppermute | solution.py:22
  874.5 0.0 collective-permute-done.3
  874.5 1.3 slice_select_fusion.1
  875.8 0.1 pad_maximum_fusion
  875.9 1.4 copy.6
  877.3 29.0 %all-to-all-start = ((f32[384,32,24]{0,2,1:T(8,128)}), f32[384,32,24]{0,2,1:T(8,128)S(1)}, u32[]{:S(2)}, u32[]{:S(2)}) async-start(f32[384,32,24]{0,2,1:T(8,128)} %bitcast.7), calls=%async_computation | async-start | bytes 2359296 | tf_op jit(solution)/shard_map/all_to_all | solution.py:91
  906.3 0.0 copy-done.4
  906.3 55.3 %all-to-all-done = f32[384,32,24]{0,2,1:T(8,128)S(1)} async-done(((f32[384,32,24]{0,2,1:T(8,128)}), f32[384,32,24]{0,2,1:T(8,128)S(1)}, u32[]{:S(2)}, u32[]{:S(2)}) %all-to-all-start) | async-done | bytes 1179680 | tf_op jit(solution)/shard_map/all_to_all | solution.py:91
  961.6 0.6 gather_fusion
  962.3 64.3 %all_to_all.10 = f32[384,32,24]{0,2,1:T(8,128)S(1)} all-to-all(f32[384,32,24]{0,2,1:T(8,128)S(1)} %bitcast.21), channel_id=1, replica_groups=mesh['row'=32,'col'=16] {'row'}, dimensions={1} | all-to-all | bytes 2359296 | tf_op jit(solution)/shard_map/all_to_all | solution.py:93
  1026.6 3.3 fusion.12
  1029.9 2.3 collective-permute-start.4
  1032.2 26.0 %collective-permute-done.4 = f32[384,768]{1,0:T(8,128)S(1)} collective-permute-done((f32[384,768]{1,0:T(8,128)S(1)}, f32[384,768]{1,0:T(8,128)S(1)}, u32[]{:S(2)}, u32[]{:S(2)}) %collective-permute-start.4) | collective-permute-done | bytes 1179680 | tf_op jit(solution)/shard_map/ppermute | solution.py:16
  1058.3 3.3 fusion.6
  1061.6 2.2 collective-permute-start.5
  1063.8 0.7 constant_dynamic-slice_fusion.3
  1065.9 23.2 %collective-permute-done.5 = f32[384,768]{1,0:T(8,128)S(1)} collective-permute-done((f32[384,768]{1,0:T(8,128)S(1)}, f32[384,768]{1,0:T(8,128)S(1)}, u32[]{:S(2)}, u32[]{:S(2)}) %collective-permute-start.5) | collective-permute-done | bytes 1179680 | tf_op jit(solution)/shard_map/ppermute | solution.py:16
  1089.1 0.1 broadcast_select_fusion.1
  1089.2 0.1 fusion.20
  1089.3 1.1 maximum_select_fusion.5
  (10 shorter events, 0.0 us)
Async XLA Ops:
  6.5 459.7 %copy-start = (f32[384,768]{1,0:T(8,128)S(1)}, f32[384,768]{1,0:T(8,128)}, u32[]{:S(2)}) copy-start(f32[384,768]{1,0:T(8,128)} %param.5) | copy-start | bytes 3538948
  6.5 232.2 %all-gather.7.cloned.1.call-start = ((), (), s32[]{:S(2)}) async-start(), calls=%async_computation.3 | async-start | bytes 2433024 | tf_op jit(solution)/shard_map/all_gather | solution.py:64
  8.2 455.6 %all-gather.5.cloned.1.call-start = ((), (), s32[]{:S(2)}) async-start(), calls=%async_computation.2 | async-start | bytes 2433024 | tf_op jit(solution)/shard_map/all_gather | solution.py:64
  9.0 780.7 %all-reduce.3.cloned.1.call-start = ((), (), s32[]{:S(2)}) async-start(), calls=%async_computation.4 | async-start | bytes 4718592 | tf_op jit(solution)/shard_map/psum | solution.py:12
  466.2 1.7 copy-start.2
  471.9 18.3 %collective-permute-start = (f32[384,768]{1,0:T(8,128)}, f32[384,768]{1,0:T(8,128)S(1)}, u32[]{:S(2)}, u32[]{:S(2)}) collective-permute-start(f32[384,768]{1,0:T(8,128)} %fusion.14), channel_id=1, source_target_pairs={{0,16},{16,0},{32,48},{48,32},{64,80},{80,64},{96,112},{112,96},{1... | collective-permute-start | bytes 3538952 | tf_op jit(solution)/shard_map/ppermute | solution.py:16
  789.7 15.7 %copy-start.3 = (s32[2,16]{1,0:T(2,128)S(1)}, s32[2,16]{1,0:T(2,128)}, u32[]{:S(2)}) copy-start(s32[2,16]{1,0:T(2,128)} %param.7) | copy-start | bytes 388
  794.8 36.9 %collective-permute-start.1 = (f32[384,768]{1,0:T(8,128)S(1)}, f32[384,768]{1,0:T(8,128)S(1)}, u32[]{:S(2)}, u32[]{:S(2)}) collective-permute-start(f32[384,768]{1,0:T(8,128)S(1)} %fusion), channel_id=1, source_target_pairs={{0,16},{16,0},{32,48},{48,32},{64,80},{80,64},{96,112},{112,96},{1... | collective-permute-start | bytes 3538952 | tf_op jit(solution)/shard_map/ppermute | solution.py:16
  832.2 42.3 %collective-permute-start.2 = (f32[384,384]{1,0:T(8,128)S(1)}, f32[384,384]{1,0:T(8,128)}, u32[]{:S(2)}, u32[]{:S(2)}) collective-permute-start(f32[384,384]{1,0:T(8,128)S(1)} %get-tuple-element.11), channel_id=1, source_target_pairs={{0,1},{1,2},{2,3},{3,4},{4,5},{5,6},{6,7},{7,8},{8,9},{9,10},{10,1... | collective-permute-start | bytes 1769480 | tf_op jit(solution)/shard_map/ppermute | solution.py:22
  834.1 40.4 %collective-permute-start.3 = (f32[384,384]{1,0:T(8,128)S(1)}, f32[384,384]{1,0:T(8,128)}, u32[]{:S(2)}, u32[]{:S(2)}) collective-permute-start(f32[384,384]{1,0:T(8,128)S(1)} %get-tuple-element.12), channel_id=1, source_target_pairs={{1,0},{2,1},{3,2},{4,3},{5,4},{6,5},{7,6},{8,7},{9,8},{10,9},{11,1... | collective-permute-start | bytes 1769480 | tf_op jit(solution)/shard_map/ppermute | solution.py:22
  877.3 29.0 %copy-start.4 = (s32[32]{0:T(128)S(1)}, s32[32]{0:T(128)}, u32[]{:S(2)}) copy-start(s32[32]{0:T(128)} %constant.66) | copy-start | bytes 388
  877.3 84.3 %all-to-all-start = ((f32[384,32,24]{0,2,1:T(8,128)}), f32[384,32,24]{0,2,1:T(8,128)S(1)}, u32[]{:S(2)}, u32[]{:S(2)}) async-start(f32[384,32,24]{0,2,1:T(8,128)} %bitcast.7), calls=%async_computation | async-start | bytes 2359296 | tf_op jit(solution)/shard_map/all_to_all | solution.py:91
  962.3 64.3 %copy-start.1 = (f32[1,1,768,768]{3,2,1,0:T(8,128)S(1)}, f32[1,1,768,768]{3,2,1,0:T(8,128)}, u32[]{:S(2)}) copy-start(f32[1,1,768,768]{3,2,1,0:T(8,128)} %all-gather.5.cloned.1.call-done) | copy-start | bytes 7077892
  1026.6 31.7 %copy-start.5 = (f32[768,384]{1,0:T(8,128)S(1)}, f32[768,384]{1,0:T(8,128)}, u32[]{:S(2)}) copy-start(f32[768,384]{1,0:T(8,128)} %get-tuple-element.5) | copy-start | bytes 3538948
  1029.9 28.4 %collective-permute-start.4 = (f32[384,768]{1,0:T(8,128)S(1)}, f32[384,768]{1,0:T(8,128)S(1)}, u32[]{:S(2)}, u32[]{:S(2)}) collective-permute-start(f32[384,768]{1,0:T(8,128)S(1)} %fusion.12), channel_id=1, source_target_pairs={{0,16},{16,0},{32,48},{48,32},{64,80},{80,64},{96,112},{112,96},{1... | collective-permute-start | bytes 3538952 | tf_op jit(solution)/shard_map/ppermute | solution.py:16
  1061.6 27.4 %collective-permute-start.5 = (f32[384,768]{1,0:T(8,128)S(1)}, f32[384,768]{1,0:T(8,128)S(1)}, u32[]{:S(2)}, u32[]{:S(2)}) collective-permute-start(f32[384,768]{1,0:T(8,128)S(1)} %fusion.6), channel_id=1, source_target_pairs={{0,16},{16,0},{32,48},{48,32},{64,80},{80,64},{96,112},{112,96},{1... | collective-permute-start | bytes 3538952 | tf_op jit(solution)/shard_map/ppermute | solution.py:16
Sparse Core Ops, SparseCore 0:
  9.4 229.2 all-gather.6
  240.9 222.9 all-gather.4
  466.8 322.7 all-reduce.2
where the time goes:
time: 1100 us
  waiting for transfers between devices  923 us (84%)
  blocking collectives  64.3 us (6%)
  starting transfers between devices  62.9 us (6%)
  between operations  16 us (1%)
  matrix products  15.8 us (1%)
    all_gather x2, waiting for transfers between devices, per_device(): whole = lax.all_gather(shard, 'row', axis=0, tiled=True)  452 us
    psum x1, waiting for transfers between devices, broadcast(): return lax.psum(kept, axis)  299 us
    ppermute x4, waiting for transfers between devices, partner_2(): lax.ppermute(value, axis, [(i, i ^ 1 << bit) for i in range(lax.axis_size...  88.3 us
    all_to_all x1, blocking collectives, per_device(): lax.all_to_all(ordered, 'row', split_axis=1, concat_axis=1, tiled=True)  64.3 us
    all_to_all x1, waiting for transfers between devices, per_device(): lax.all_to_all(sliced, 'row', split_axis=1, concat_axis=1, tiled=True)  55.3 us
    all_to_all x1, starting transfers between devices, per_device(): lax.all_to_all(sliced, 'row', split_axis=1, concat_axis=1, tiled=True)  29 us
    ppermute x2, waiting for transfers between devices, from_behind(): return lax.ppermute(block, axis, route)  27.1 us
  transfers between devices with their start and end apart: 10, of which 9 were waited for; matrix products, arithmetic and copies ran while one was open for 1% of the time, Pallas kernels for 0%

commit v1 on v0

v1 whole, which is shorter than its diff:
```python
import functools

import jax
import jax.numpy as jnp
from jax import lax
from jax.experimental import pallas as pl
from jax.experimental.pallas import tpu as pltpu
from jax.sharding import PartitionSpec as P

ROUNDS = 2
ORDER = 384
PAIR = 768
LAYERS = 8
SIDES = 4
PIECE = 24
MESH = pl.DeviceIdType.MESH


def split(value):
    high = value.astype(jnp.bfloat16)
    return high, (value - high.astype(jnp.float32)).astype(jnp.bfloat16)


def product(first, second):
    one = functools.partial(jnp.dot, preferred_element_type=jnp.float32)
    return one(first[0], second[0]) + (one(first[0], second[1]) + one(first[1], second[0]))


def moved_to(place):
    even = jnp.where(place == 0, 0, jnp.where(place == 30, 31, place + 2))
    return jnp.where(place % 2 == 0, even, jnp.where(place == 1, 2, place - 2))


def came_from(place):
    even = jnp.where(place == 0, 0, jnp.where(place == 2, 1, place - 2))
    return jnp.where(place % 2 == 0, even, jnp.where(place == 31, 30, place + 2))


def crosses(place):
    edge = place % 4
    return ((edge == 0) & (place != 0)) | ((edge == 3) & (place != 31))


def kernel(
    tile, turn, out, right, left, other, fresh, block, flipped, left_high, left_low, mid_high,
    mid_low, own_sem, other_sem, right_sem, left_sem, spread_sem, fresh_sem, chain_out, side_out,
    relay_out, left_out, spread_out, other_out, block_out, flipped_out, pass_out,
):
    row, col = lax.axis_index("row"), lax.axis_index("col")
    layer, side = row // SIDES, row % SIDES
    along, far, core = col // 4, (col // 2) % 2, col % 2
    parity = row % 2
    group = along * 2 + core
    partner = layer * SIDES + (side + 1 - 2 * parity)
    beside = layer * SIDES + (SIDES - 1 - side)
    has_down, has_up = layer > 0, layer < LAYERS - 1
    down, up = row - SIDES, row + SIDES

    place = moved_to(row)
    sends_flipped = crosses(place)
    main = jnp.where(col == 0, 1, core)
    edge_col = (col == 0) | (col == 15)
    mate_col = col + 1 - 2 * core
    mate_place = place + 1 - 2 * (place % 2)

    def left_target(half, reach):
        return (2 * col + half, 4 * (layer // 2) + 2 * reach + layer % 2)

    def left_source(index):
        return (SIDES * group + index, row // 2)

    def peer(step):
        number = (group + step) % 8
        return (row, 4 * (number // 2) + 2 * far + number % 2)

    def same(device):
        return (device[0] == row) & (device[1] == col)

    barrier = pltpu.get_barrier_semaphore()

    def greet(device):
        pl.semaphore_signal(barrier, inc=1, device_id=device, device_id_type=MESH)

    expected = 2 + 7
    greet((partner, col))
    greet((beside, col))
    for step in range(1, 8):
        greet(peer(step))
    pl.when(has_down)(lambda: greet((down, col)))
    pl.when(has_up)(lambda: greet((up, col)))
    expected += has_down.astype(jnp.int32) + has_up.astype(jnp.int32)
    for index in range(SIDES):
        device = left_source(index)
        pl.when(jnp.logical_not(same(device)))(functools.partial(greet, device))
    for half in range(2):
        for reach in range(2):
            expected += 1 - same(left_target(half, reach)).astype(jnp.int32)
    row_source = came_from(row)
    partner_source = came_from(partner)
    greet((row_source, mate_col))
    greet((partner_source, mate_col))
    expected += 2
    for origin in (row_source, partner_source):
        pl.when(edge_col & (origin != row))(functools.partial(greet, (origin, col)))
    for target in (place, mate_place):
        expected += (edge_col & (target != row)).astype(jnp.int32)
    far_place = 2 * col + core
    pl.when(jnp.logical_not(edge_col))(lambda: greet((came_from(far_place), row_source // 2)))
    expected += 2 * sends_flipped.astype(jnp.int32)
    pl.semaphore_wait(barrier, expected)

    def remote(source, target, send_sem, recv_sem, device):
        return pltpu.make_async_remote_copy(
            src_ref=source, dst_ref=target, send_sem=send_sem, recv_sem=recv_sem,
            device_id=device, device_id_type=MESH,
        )

    def arrived(ref, sem):
        remote(ref, ref, sem, sem, (partner, col)).wait_recv()

    def left_copy(half, reach):
        return remote(
            turn.at[:, :, pl.ds(half * ORDER, ORDER)], left.at[:, layer, side],
            left_out.at[half, reach], left_sem.at[side], left_target(half, reach),
        )

    for half in range(2):
        for reach in range(2):
            is_self = same(left_target(half, reach))

            @pl.when(is_self)
            def _():
                pltpu.make_async_copy(
                    turn.at[:, :, pl.ds(half * ORDER, ORDER)], left.at[:, layer, side],
                    left_sem.at[side],
                ).start()

            pl.when(jnp.logical_not(is_self))(left_copy(half, reach).start)

    def side_copy(source, number, which):
        return remote(
            source, right.at[:, number, side], side_out.at[number, which],
            right_sem.at[number, side], (beside if which else partner, col),
        )

    partner_side = side + 1 - 2 * parity

    def relay_copy(number):
        slot = right.at[:, number, partner_side]
        return remote(
            slot, slot, relay_out.at[number], right_sem.at[number, partner_side], (beside, col)
        )

    def up_copy(source, number):
        return remote(
            source, right.at[:, number, side], chain_out.at[number, 0],
            right_sem.at[number, side], (up, col),
        )

    def down_copy(source, number):
        return remote(
            source, right.at[:, number, side], chain_out.at[number, 1],
            right_sem.at[number, side], (down, col),
        )

    pl.when(has_up)(lambda: up_copy(turn, layer).start())
    pl.when(has_down)(lambda: down_copy(turn, layer).start())
    for which in range(2):
        side_copy(turn, layer, which).start()
    other_copy = remote(tile, other, other_out, other_sem, (partner, col))
    other_copy.start()
    own_copy = pltpu.make_async_copy(turn, right.at[:, layer, side], own_sem)
    own_copy.start()

    def spread_copy(step):
        return remote(
            left.at[:, group], left.at[:, group], spread_out.at[step], spread_sem.at[group],
            peer(step),
        )

    for index in range(SIDES):
        arrived(left.at[:, group, index], left_sem.at[index])
    for step in range(1, 8):
        spread_copy(step).start()

    def relay(number):
        arrived(right.at[:, number, partner_side], right_sem.at[number, partner_side])
        relay_copy(number).start()

    relay(layer)

    @pl.loop(0, LAYERS - 1)
    def _(step):
        lower, upper = layer - 1 - step, layer + 1 + step

        @pl.when(lower >= 0)
        def _():
            slot = right.at[:, lower, side]
            arrived(slot, right_sem.at[lower, side])
            pl.when(has_up)(lambda: up_copy(slot, lower).start())
            side_copy(slot, lower, 1).start()
            side_copy(slot, lower, 0).start()

        @pl.when(upper < LAYERS)
        def _():
            slot = right.at[:, upper, side]
            arrived(slot, right_sem.at[upper, side])
            pl.when(has_down)(lambda: down_copy(slot, upper).start())
            side_copy(slot, upper, 1).start()
            side_copy(slot, upper, 0).start()

        pl.when(lower >= 0)(lambda: relay(lower))
        pl.when(upper < LAYERS)(lambda: relay(upper))

    for step in range(1, 8):
        number = (group + step) % 8
        arrived(left.at[:, number], spread_sem.at[number])
    for turn_index in range(ROUNDS):
        for half in range(2):
            part = left[turn_index, 4 * half:4 * half + 4].reshape(ORDER, ORDER)
            high, low = split(part.T)
            left_high[turn_index, half] = high
            left_low[turn_index, half] = low

    def left_of(turn_index, half):
        return left_high[turn_index, half], left_low[turn_index, half]

    arrived(other, other_sem)

    @pl.loop(0, 3)
    def _(step):
        columns = pl.ds(pl.multiple_of(step * 256, 256), 256)
        total = product(left_of(0, parity), split(tile[:, columns]))
        total += product(left_of(0, 1 - parity), split(other[:, columns]))
        mid_high[:, columns], mid_low[:, columns] = split(total)

    own_copy.wait()

    @pl.loop(0, LAYERS)
    def _(number):
        arrived(right.at[:, number, beside % SIDES], right_sem.at[number, beside % SIDES])
        opposite = (side + 2) % SIDES
        arrived(right.at[:, number, opposite], right_sem.at[number, opposite])

    def block_copy(half, which):
        target = mate_place if which else place
        slot = jnp.where(col == 0, 0, core)
        index = place % 2
        return remote(
            block.at[half], fresh.at[index, slot], block_out.at[0, which],
            fresh_sem.at[index, slot], (target, mate_col),
        )

    def edge_copy(half, which):
        target = mate_place if which else place
        slot = jnp.where(col == 0, 0, 1)
        index = place % 2
        return remote(
            block.at[half], fresh.at[index, slot], block_out.at[1, which],
            fresh_sem.at[index, slot], (target, col),
        )

    def flipped_copy(half):
        target = moved_to(2 * col + half)
        return remote(
            flipped.at[half], fresh.at[target % 2, place % 2], flipped_out.at[half],
            fresh_sem.at[target % 2, place % 2], (target, place // 2),
        )

    def is_self(which):
        return (mate_place if which else place) == row

    for half in range(2):
        on_edge = edge_col & (main != half)

        @pl.when((main == half) | edge_col | sends_flipped)
        def _():
            columns = pl.ds(half * ORDER, ORDER)
            turned = right[0, :, :, :, columns].reshape(PAIR, ORDER)
            value = product((mid_high[...], mid_low[...]), split(turned))
            block[half] = value

            @pl.when(sends_flipped)
            def _():
                flipped[half] = value.T
                flipped_copy(half).start()

            @pl.when(main == half)
            def _():
                block_copy(half, 0).start()
                block_copy(half, 1).start()

            for which in range(2):
                pl.when(on_edge & jnp.logical_not(is_self(which)))(edge_copy(half, which).start)

                @pl.when(on_edge & is_self(which))
                def _():
                    slot = jnp.where(col == 0, 0, 1)
                    pltpu.make_async_copy(
                        block.at[half], fresh.at[place % 2, slot],
                        fresh_sem.at[place % 2, slot],
                    ).start()

    far_slot = jnp.where(col == 0, 1, jnp.where(col == 15, 0, core))
    near_slot = 1 - far_slot
    inner = jnp.logical_not(edge_col)

    def arrive_fresh(index, slot):
        arrived(fresh.at[index, slot], fresh_sem.at[index, slot])

    def second_left(slot):
        total = product(left_of(1, 0), split(fresh[0, slot]))
        total += product(left_of(1, 1), split(fresh[1, slot]))
        columns = pl.ds(pl.multiple_of(slot * ORDER, 128), ORDER)
        mid_high[:, columns], mid_low[:, columns] = split(total)

    arrive_fresh(parity, near_slot)
    arrive_fresh(1 - parity, near_slot)
    second_left(near_slot)
    arrive_fresh(parity, far_slot)
    pass_copy = remote(
        fresh.at[parity, far_slot], fresh.at[parity, far_slot], pass_out,
        fresh_sem.at[parity, far_slot], (partner, col),
    )
    pl.when(inner)(pass_copy.start)
    arrive_fresh(1 - parity, far_slot)
    second_left(far_slot)

    @pl.loop(0, 3)
    def _(step):
        columns = pl.ds(pl.multiple_of(step * 256, 256), 256)
        turned = right[1, :, :, :, columns].reshape(PAIR, 256)
        out[:, columns] = product((mid_high[...], mid_low[...]), split(turned))

    for half in range(2):
        for reach in range(2):
            device = left_target(half, reach)
            pl.when(jnp.logical_not(same(device)))(left_copy(half, reach).wait_send)
    for step in range(1, 8):
        spread_copy(step).wait_send()

    @pl.loop(0, LAYERS)
    def _(number):
        slot = right.at[:, number, side]
        pl.when(has_up & (number <= layer))(lambda: up_copy(slot, number).wait_send())
        pl.when(has_down & (number >= layer))(lambda: down_copy(slot, number).wait_send())
        side_copy(slot, number, 0).wait_send()
        side_copy(slot, number, 1).wait_send()
        relay_copy(number).wait_send()

    other_copy.wait_send()
    for half in range(2):
        pl.when(sends_flipped)(flipped_copy(half).wait_send)
    for which in range(2):
        block_copy(0, which).wait_send()
        pl.when(edge_col & jnp.logical_not(is_self(which)))(edge_copy(0, which).wait_send)
    pl.when(inner)(pass_copy.wait_send)


def per_device(covariance, rotations, flips):
    shard = rotations[:, 0]
    own_flip = flips[:, lax.axis_index("col")]
    traded = jnp.concatenate([shard[:, :, ORDER:], shard[:, :, :ORDER]], 2)
    turn = jnp.where((own_flip == 1)[:, None, None], traded, shard)
    dma = pltpu.SemaphoreType.DMA
    return pl.pallas_call(
        kernel,
        out_shape=jax.ShapeDtypeStruct((ORDER, PAIR), jnp.float32),
        in_specs=[pl.BlockSpec(memory_space=pltpu.VMEM)] * 2,
        out_specs=pl.BlockSpec(memory_space=pltpu.VMEM),
        scratch_shapes=[
            pltpu.VMEM((ROUNDS, LAYERS, SIDES, PIECE, PAIR), jnp.float32),
            pltpu.VMEM((ROUNDS, LAYERS, SIDES, PIECE, ORDER), jnp.float32),
            pltpu.VMEM((ORDER, PAIR), jnp.float32),
            pltpu.VMEM((2, 2, ORDER, ORDER), jnp.float32),
            pltpu.VMEM((2, ORDER, ORDER), jnp.float32),
            pltpu.VMEM((2, ORDER, ORDER), jnp.float32),
            pltpu.VMEM((ROUNDS, 2, ORDER, ORDER), jnp.bfloat16),
            pltpu.VMEM((ROUNDS, 2, ORDER, ORDER), jnp.bfloat16),
            pltpu.VMEM((ORDER, PAIR), jnp.bfloat16),
            pltpu.VMEM((ORDER, PAIR), jnp.bfloat16),
            dma,
            dma,
            dma((LAYERS, SIDES)),
            dma((SIDES,)),
            dma((LAYERS,)),
            dma((2, 2)),
            dma((LAYERS, 2)),
            dma((LAYERS, 2)),
            dma((LAYERS,)),
            dma((2, 2)),
            dma((8,)),
            dma,
            dma((2, 2)),
            dma((2,)),
            dma,
        ],
        compiler_params=pltpu.CompilerParams(
            collective_id=0, has_side_effects=True, vmem_limit_bytes=48 * 2**20
        ),
        cost_estimate=pl.CostEstimate(
            flops=12 * ORDER * PAIR * PAIR, bytes_accessed=3 * 2**20, transcendentals=0
        ),
    )(covariance, turn)


def solution(mesh):
    placed = (P("row", "col"), P(None, "col", "row", None), P())
    return jax.shard_map(
        per_device, mesh=mesh, in_specs=placed, out_specs=P("row", "col"), check_vma=False
    )
```

time: 1100 us -> 245 us (0.22)
  the two profiles are of different devices: /device:TPU:2 before, /device:TPU:422 now
where the time goes in v1:
time: 245 us
  Pallas kernels  240 us (98%)
  local copies, waits for them, and re-layouts  3.21 us (1%)
    pallas_call x1, Pallas kernels, per_device(): pl.pallas_call(kernel, out_shape=jax.ShapeDtypeStruct((ORDER, PAIR), jnp....  240 us

profile of v1, /device:TPU:422, one launch (start us, length us, event | category | flops | bytes accessed | tf_op | source)
XLA Modules:
  0.0 245.2 jit_solution(5248787793250103878)
XLA Ops:
  0.0 0.9 compare_reduce_fusion
  0.9 0.9 fusion
  1.8 1.0 maximum_select_fusion.turn
  2.8 0.0 copy-start
  2.8 1.3 copy-done
  4.1 240.1 %shard_map.37 = f32[384,768]{1,0:T(8,128)S(1)} custom-call(f32[384,768]{1,0:T(8,128)S(1)} %copy-done, f32[2,24,768]{2,1,0:T(8,128)S(1)} %maximum_select_fusion.turn), custom_call_target="tpu_custom_call" | custom-call | flops 2717908992 | bytes 3145728 | tf_op jit(solution)/shard_map/pallas_call | solution.py:366
  244.1 1.0 copy.5
Async XLA Ops:
  2.8 1.3 copy-start

commit v2 on v0

v2 whole, which is shorter than its diff:
```python
import functools

import jax
import jax.numpy as jnp
from jax import lax
from jax.experimental import pallas as pl
from jax.experimental.pallas import tpu as pltpu
from jax.sharding import PartitionSpec as P

ROUNDS = 2
ORDER = 384
PAIR = 768
LAYERS = 8
SIDES = 4
PIECE = 24
CHUNKS = 4
CHUNK = 96
MESH = pl.DeviceIdType.MESH


def split(value):
    high = value.astype(jnp.bfloat16)
    return high, (value - high.astype(jnp.float32)).astype(jnp.bfloat16)


def product(first, second):
    one = functools.partial(jnp.dot, preferred_element_type=jnp.float32)
    return one(first[0], second[0]) + (one(first[0], second[1]) + one(first[1], second[0]))


def moved_to(place):
    even = jnp.where(place == 0, 0, jnp.where(place == 30, 31, place + 2))
    return jnp.where(place % 2 == 0, even, jnp.where(place == 1, 2, place - 2))


def came_from(place):
    even = jnp.where(place == 0, 0, jnp.where(place == 2, 1, place - 2))
    return jnp.where(place % 2 == 0, even, jnp.where(place == 31, 30, place + 2))


def kernel(
    tile, turn, out, right, left, both, fresh, block, stage, left_high, left_low, mid_high,
    mid_low, passing, tile_sem, own_sem, pair_sem, right_sem, left_sem, mirror_sem, spread_sem, both_sem,
    fresh_sem, passing_sem,
    out_sem, left_out, mirror_out, spread_out, pair_out, both_out, chain_out, across_out,
    mate_out, mate_both_out, block_out, mate_fresh_out, final_out, passing_out,
):
    row, col = lax.axis_index("row"), lax.axis_index("col")
    layer, side = row // SIDES, row % SIDES
    along, far, core = col // 4, (col // 2) % 2, col % 2
    parity, half_side = row % 2, side // 2
    pair, target_pair = row // 2, 2 * (col // 2) + parity
    is_main = core == parity
    is_helper = core != parity
    mate_col = col + 1 - 2 * core
    partner_row = row + 1 - 2 * parity
    across_row = layer * SIDES + (side + 2) % SIDES
    has_down, has_up = layer > 0, layer < LAYERS - 1
    down, up = row - SIDES, row + SIDES
    mate, partner, across = (row, mate_col), (partner_row, col), (across_row, col)
    diagonal = (partner_row, mate_col)

    def same(device):
        return (device[0] == row) & (device[1] == col)

    def left_target(half, reach):
        return (2 * col + layer % 2, 4 * (layer // 2) + 2 * reach + half)

    def left_source(index):
        return (SIDES * (2 * along + parity) + index, pair)

    def peer(step):
        return (row, (col + 4 * step) % 16)

    far_half = jnp.where(target_pair % 2 == 0, 1, 0)
    far_slot = 1 - far_half

    def inside(pair_col):
        return (pair_col != 0) & (pair_col != 15)

    def target_of(old_row, old_col):
        new_row, new_col = moved_to(old_row), moved_to(old_col)
        pair_col = new_col // 2
        return (2 * (new_row // 2) + pair_col % 2, 2 * (pair_col // 2) + new_row % 2)

    def relayed(old_row, pair_col, is_far):
        return is_far & inside(pair_col) & (old_row % 2 == (old_row // 2) % 2)

    def turned_layer(number, half_z):
        wraps = (number < 0) | (number >= LAYERS)
        return (number + LAYERS) % LAYERS, jnp.where(wraps, 1 - half_z, half_z)

    def relay_of(old_row, pair_col):
        odd = (old_row // 2) % 2
        number, half_z = turned_layer(old_row // 4 + 2 * odd - 1, (pair_col // 2) % 2)
        return (
            number * SIDES + 2 * odd + pair_col % 2,
            4 * (pair_col // 4) + 2 * half_z + 1 - pair_col % 2,
        )

    def block_target(half):
        old_row = 2 * pair + core
        end = target_of(old_row, 2 * target_pair + half)
        through = relayed(old_row, target_pair, half == far_half)
        stop = relay_of(old_row, target_pair)
        return tuple(jnp.where(through, one, other) for one, other in zip(stop, end))

    def block_source(slot):
        old_row, old_col = came_from(2 * pair + core), came_from(2 * target_pair + slot)
        pair_col = old_col // 2
        start = (2 * (old_row // 2) + pair_col % 2, 2 * (pair_col // 2) + old_row % 2)
        far = jnp.where(pair_col % 2 == 0, 1, 0)
        through = relayed(old_row, pair_col, old_col % 2 == far)
        stop = relay_of(old_row, pair_col)
        return tuple(jnp.where(through, one, other) for one, other in zip(stop, start))

    relay_layer, relay_far = turned_layer(layer + 1 - 2 * half_side, far)
    relay_pair, relay_col = 2 * relay_layer + half_side, 4 * along + 2 * relay_far + parity
    relays = is_helper & inside(relay_col)
    relay_source = (relay_layer * SIDES + side, 4 * along + 2 * relay_far + half_side)
    own_row = 2 * pair + core
    uses_relay = relayed(own_row, target_pair, jnp.bool_(True))
    relay_old = (2 * relay_pair + half_side, 2 * relay_col + far_half)
    relay_target = target_of(*relay_old)

    barrier = pltpu.get_barrier_semaphore()

    def greet(device, when=None):
        def signal():
            pl.semaphore_signal(barrier, inc=1, device_id=device, device_id_type=MESH)

        if when is None:
            signal()
        else:
            pl.when(when)(signal)

    def count(flag):
        return flag.astype(jnp.int32)

    expected = 6
    for device in (mate, partner, across, peer(1), peer(2), peer(3)):
        greet(device)
    for device, when in (
        (diagonal, is_helper), ((up, col), has_up), ((down, col), has_down)
    ):
        greet(device, when)
        expected += count(when)
    for index in range(SIDES):
        device = left_source(index)
        greet(device, jnp.logical_not(same(device)))
    for half in range(2):
        for reach in range(2):
            expected += 1 - count(same(left_target(half, reach)))
    for slot in range(2):
        device = block_source(slot)
        greet(device, jnp.logical_not(same(device)))
        expected += 1 - count(same(block_target(slot)))
    greet(relay_source, relays)
    expected += count(relays)
    pl.semaphore_wait(barrier, expected)

    def remote(source, target, send_sem, recv_sem, device):
        return pltpu.make_async_remote_copy(
            src_ref=source, dst_ref=target, send_sem=send_sem, recv_sem=recv_sem,
            device_id=device, device_id_type=MESH,
        )

    def arrived(ref, sem):
        remote(ref, ref, sem, sem, partner).wait_recv()

    def left_piece(index, half):
        return turn.at[index, half]

    def left_copy(index, half, reach):
        return remote(
            left_piece(index, half), left.at[index, layer, side], left_out.at[index, half, reach],
            left_sem.at[index, side], left_target(half, reach),
        )

    def left_start(index):
        for half in range(2):
            for reach in range(2):
                here = same(left_target(half, reach))
                pl.when(here)(
                    pltpu.make_async_copy(
                        left_piece(index, half), left.at[index, layer, side],
                        left_sem.at[index, side],
                    ).start
                )
                pl.when(jnp.logical_not(here))(left_copy(index, half, reach).start)

    group = 2 * along + parity

    def mirror_copy(index):
        slot = left.at[index, group]
        return remote(slot, slot, mirror_out.at[index], mirror_sem.at[index], partner)

    def spread_copy(index, which, step):
        number = 2 * along + (parity if which == 0 else 1 - parity)
        slot = left.at[index, number]
        return remote(
            slot, slot, spread_out.at[index, which, step], spread_sem.at[index, number], peer(step)
        )

    def left_mirror(index):
        for number in range(SIDES):
            arrived(left.at[index, group, number], left_sem.at[index, number])
        mirror_copy(index).start()
        for step in range(1, 4):
            spread_copy(index, 0, step).start()

    def left_spread(index):
        arrived(left.at[index, 2 * along + 1 - parity], mirror_sem.at[index])
        for step in range(1, 4):
            spread_copy(index, 1, step).start()

    def left_finish(index):
        for step in range(1, 4):
            for which in range(2):
                number = 2 * ((along + step) % 4) + which
                arrived(left.at[index, number], spread_sem.at[index, number])
        for half in range(2):
            part = left[index, 4 * half:4 * half + 4].reshape(ORDER, ORDER)
            left_high[index, half], left_low[index, half] = split(part.T)

    def slot_of(index, half, number, which):
        return right.at[1, :, number, which] if index else right.at[0, half, number, which]

    def piece_slot(index, half, which):
        rows = pl.ds(pl.multiple_of(PIECE * which, 8), PIECE)
        if index:
            return right.at[1, :, layer, half_side, rows]
        return right.at[0, half, layer, half_side, rows]

    def chunk(ref, index, number):
        return ref.at[index, pl.ds(number * CHUNK, CHUNK)]

    def pair_copy(half):
        return remote(
            turn.at[0, half], piece_slot(0, half, parity), pair_out.at[half], pair_sem.at[half],
            partner,
        )

    def later_copy(device, number):
        return remote(
            turn.at[1], piece_slot(1, 0, parity), pair_out.at[2], pair_sem.at[2 + number], device
        )

    to_mate, to_diagonal = later_copy(mate, 0), later_copy(diagonal, 1)

    def own_piece(half):
        return pltpu.make_async_copy(
            turn.at[0, half], piece_slot(0, half, parity), own_sem.at[half]
        )

    own_tile = pltpu.make_async_copy(tile, both.at[parity], tile_sem)
    mate_tile = remote(tile, both.at[parity], mate_both_out.at[CHUNKS], both_sem.at[CHUNKS], mate)

    def both_copy(number):
        return remote(
            tile.at[pl.ds(number * CHUNK, CHUNK)], chunk(both, parity, number),
            both_out.at[number], both_sem.at[number], partner,
        )

    def mate_both(number):
        slot = chunk(both, 1 - parity, number)
        return remote(slot, slot, mate_both_out.at[number], both_sem.at[number], mate)

    def toward(index, half, number, which, sem, device):
        slot = slot_of(index, half, number, which)
        return remote(slot, slot, sem, right_sem.at[index, half, number, which], device)

    def up_copy(index, half, number):
        return toward(
            index, half, number, half_side, chain_out.at[index, half, number, 0], (up, col)
        )

    def down_copy(index, half, number):
        return toward(
            index, half, number, half_side, chain_out.at[index, half, number, 1], (down, col)
        )

    def across_copy(index, half, number):
        return toward(index, half, number, half_side, across_out.at[index, half, number], across)

    def mate_copy(index, half, number, which):
        return toward(index, half, number, which, mate_out.at[index, half, number, which], mate)

    def wait_right(index, half, number, which):
        arrived(slot_of(index, half, number, which), right_sem.at[index, half, number, which])

    halves = (far_half, 1 - far_half)

    def chain_send(index, half):
        pl.when(has_up)(lambda: up_copy(index, half, layer).start())
        pl.when(has_down)(lambda: down_copy(index, half, layer).start())
        across_copy(index, half, layer).start()
        mate_copy(index, half, layer, half_side).start()

    def chain_step(index, half, step):
        lower, upper = layer - 1 - step, layer + 1 + step

        @pl.when(lower >= 0)
        def _():
            wait_right(index, half, lower, half_side)
            pl.when(has_up)(lambda: up_copy(index, half, lower).start())
            across_copy(index, half, lower).start()
            mate_copy(index, half, lower, half_side).start()

        @pl.when(upper < LAYERS)
        def _():
            wait_right(index, half, upper, half_side)
            pl.when(has_down)(lambda: down_copy(index, half, upper).start())
            across_copy(index, half, upper).start()
            mate_copy(index, half, upper, half_side).start()

    def chain_finish(index, half):
        leads, follows = (is_helper, is_main) if index else (is_main, is_helper)

        @pl.when(leads)
        def _():
            @pl.loop(0, LAYERS)
            def _(number):
                wait_right(index, half, number, 1 - half_side)
                mate_copy(index, half, number, 1 - half_side).start()

        @pl.when(follows)
        def _():
            @pl.loop(0, LAYERS)
            def _(number):
                wait_right(index, half, number, 0)
                wait_right(index, half, number, 1)

    @pl.when(is_helper)
    def _():
        for half in halves:
            pair_copy(half).start()

    left_start(0)

    @pl.when(is_helper)
    def _():
        for number in range(CHUNKS):
            both_copy(number).start()
        to_diagonal.start()
        arrived(piece_slot(1, 0, parity), pair_sem.at[2])
        arrived(piece_slot(1, 0, 1 - parity), pair_sem.at[3])
        chain_send(1, 0)

    @pl.when(is_main)
    def _():
        to_mate.start()
        for half in halves:
            own_piece(half).start()
        for half in halves:
            own_piece(half).wait()
            arrived(piece_slot(0, half, 1 - parity), pair_sem.at[half])
            chain_send(0, half)
        own_tile.start()
        mate_tile.start()

    @pl.loop(0, LAYERS - 1)
    def _(step):
        @pl.when(is_main)
        def _():
            @pl.loop(0, 2)
            def _(turn_half):
                half = jnp.where(turn_half == 0, far_half, 1 - far_half)
                chain_step(0, half, step)

        pl.when(is_helper)(lambda: chain_step(1, 0, step))
        pl.when(step == 2)(lambda: left_mirror(0))
        pl.when(step == 4)(lambda: left_spread(0))

        @pl.when(is_main & (step >= 3))
        def _():
            number = step - 3
            arrived(chunk(both, 1 - parity, number), both_sem.at[number])
            mate_both(number).start()

    left_start(1)

    left_finish(0)

    def left_of(index, half):
        return left_high[index, half], left_low[index, half]

    pl.when(is_main)(own_tile.wait)

    @pl.when(is_helper)
    def _():
        arrived(both.at[parity], both_sem.at[CHUNKS])
        for number in range(CHUNKS):
            arrived(chunk(both, 1 - parity, number), both_sem.at[number])

    @pl.loop(0, 3)
    def _(step):
        columns = pl.ds(pl.multiple_of(step * 256, 256), 256)
        total = product(left_of(0, 0), split(both[0, :, columns]))
        total += product(left_of(0, 1), split(both[1, :, columns]))
        mid_high[:, columns], mid_low[:, columns] = split(total)

    def block_ends(half):
        new_row, new_col = moved_to(2 * pair + core), moved_to(2 * target_pair + half)
        index, slot = new_row % 2, new_col % 2
        return block.at[half], fresh.at[index, slot], fresh_sem.at[index, slot]

    def block_copy(half):
        source, target, sem = block_ends(half)
        return remote(source, target, block_out.at[half, 0], sem, block_target(half))

    def relayed_copy(number):
        rows = pl.ds(number * CHUNK, CHUNK)
        return remote(
            block.at[far_half, rows], passing.at[rows], block_out.at[far_half, number],
            passing_sem.at[number], block_target(far_half),
        )

    def passing_copy(number):
        rows = pl.ds(number * CHUNK, CHUNK)
        index, slot = moved_to(relay_old[0]) % 2, moved_to(relay_old[1]) % 2
        return remote(
            passing.at[rows], fresh.at[index, slot, rows], passing_out.at[number],
            fresh_sem.at[index, slot], relay_target,
        )

    @pl.loop(0, 2)
    def _(step):
        half = jnp.where(step == 0, far_half, 1 - far_half)
        chain_finish(0, half)
        turned = right[0, half].reshape(PAIR, ORDER)
        block[half] = product((mid_high[...], mid_low[...]), split(turned))
        here = same(block_target(half))
        through = uses_relay & (half == far_half)

        @pl.when(through)
        def _():
            for number in range(CHUNKS):
                relayed_copy(number).start()

        plain = jnp.logical_not(here) & jnp.logical_not(through)
        pl.when(plain)(lambda: block_copy(half).start())
        pl.when(here)(lambda: pltpu.make_async_copy(*block_ends(half)).start())

    @pl.when(relays)
    def _():
        for number in range(CHUNKS):
            arrived(passing.at[pl.ds(number * CHUNK, CHUNK)], passing_sem.at[number])
            passing_copy(number).start()

    left_mirror(1)
    left_spread(1)
    chain_finish(1, 0)
    left_finish(1)

    def arrive_fresh(index, slot):
        arrived(fresh.at[index, slot], fresh_sem.at[index, slot])

    def mate_fresh(slot):
        ref = fresh.at[core, slot]
        return remote(ref, ref, mate_fresh_out.at[slot], fresh_sem.at[core, slot], mate)

    @pl.loop(0, 2)
    def _(step):
        slot = jnp.where(step == 0, 1 - far_slot, far_slot)
        arrive_fresh(core, slot)
        mate_fresh(slot).start()
        arrive_fresh(1 - core, slot)
        total = product(left_of(1, 0), split(fresh[0, slot]))
        total += product(left_of(1, 1), split(fresh[1, slot]))
        columns = pl.ds(pl.multiple_of(slot * ORDER, 128), ORDER)
        mid_high[:, columns], mid_low[:, columns] = split(total)

    def final_copy(number):
        columns = pl.ds(number * ORDER, ORDER)
        return remote(
            stage.at[:, columns], out.at[:, columns], final_out.at[number], out_sem.at[number],
            diagonal,
        )

    for number in range(2):
        columns = pl.ds(number * ORDER, ORDER)
        turned = right[1, number].reshape(PAIR, ORDER)
        value = product((mid_high[...], mid_low[...]), split(turned))

        @pl.when(is_main)
        def _():
            out[:, columns] = value

        @pl.when(is_helper)
        def _():
            stage[:, columns] = value
            final_copy(number).start()

    for index in range(ROUNDS):
        for half in range(2):
            for reach in range(2):
                device = left_target(half, reach)
                pl.when(jnp.logical_not(same(device)))(left_copy(index, half, reach).wait_send)
        mirror_copy(index).wait_send()
        for step in range(1, 4):
            spread_copy(index, 0, step).wait_send()
            spread_copy(index, 1, step).wait_send()
    for half in range(2):
        through = uses_relay & (half == far_half)
        plain = jnp.logical_not(same(block_target(half))) & jnp.logical_not(through)
        pl.when(plain)(block_copy(half).wait_send)
        mate_fresh(half).wait_send()

    @pl.when(is_helper)
    def _():
        for half in range(2):
            pair_copy(half).wait_send()
        to_diagonal.wait_send()
        for number in range(CHUNKS):
            both_copy(number).wait_send()

    @pl.when(is_main)
    def _():
        mate_tile.wait_send()
        for number in range(CHUNKS):
            mate_both(number).wait_send()

        to_mate.wait_send()

    def chain_left(index, half):
        @pl.loop(0, LAYERS)
        def _(number):
            rises, falls = has_up & (number <= layer), has_down & (number >= layer)
            pl.when(rises)(lambda: up_copy(index, half, number).wait_send())
            pl.when(falls)(lambda: down_copy(index, half, number).wait_send())
            across_copy(index, half, number).wait_send()
            mate_copy(index, half, number, 0).wait_send()
            mate_copy(index, half, number, 1).wait_send()

    pl.when(is_main)(lambda: chain_left(0, 0))
    pl.when(is_main)(lambda: chain_left(0, 1))
    pl.when(is_helper)(lambda: chain_left(1, 0))

    for number in range(CHUNKS):
        pl.when(uses_relay)(relayed_copy(number).wait_send)
        pl.when(relays)(passing_copy(number).wait_send)

    @pl.when(is_helper)
    def _():
        for number in range(2):
            arrived(out.at[:, pl.ds(number * ORDER, ORDER)], out_sem.at[number])
            final_copy(number).wait_send()


def per_device(covariance, rotations, flips):
    shard = rotations[:, 0]
    own_flip = flips[:, lax.axis_index("col")]
    halves = jnp.stack([shard[:, :, :ORDER], shard[:, :, ORDER:]], 1)
    turn = jnp.where((own_flip == 1)[:, None, None, None], halves[:, ::-1], halves)
    dma = pltpu.SemaphoreType.DMA
    return pl.pallas_call(
        kernel,
        out_shape=jax.ShapeDtypeStruct((ORDER, PAIR), jnp.float32),
        in_specs=[pl.BlockSpec(memory_space=pltpu.VMEM)] * 2,
        out_specs=pl.BlockSpec(memory_space=pltpu.VMEM),
        scratch_shapes=[
            pltpu.VMEM((ROUNDS, 2, LAYERS, 2, 2 * PIECE, ORDER), jnp.float32),
            pltpu.VMEM((ROUNDS, LAYERS, SIDES, PIECE, ORDER), jnp.float32),
            pltpu.VMEM((2, ORDER, PAIR), jnp.float32),
            pltpu.VMEM((2, 2, ORDER, ORDER), jnp.float32),
            pltpu.VMEM((2, ORDER, ORDER), jnp.float32),
            pltpu.VMEM((ORDER, PAIR), jnp.float32),
            pltpu.VMEM((ROUNDS, 2, ORDER, ORDER), jnp.bfloat16),
            pltpu.VMEM((ROUNDS, 2, ORDER, ORDER), jnp.bfloat16),
            pltpu.VMEM((ORDER, PAIR), jnp.bfloat16),
            pltpu.VMEM((ORDER, PAIR), jnp.bfloat16),
            pltpu.VMEM((ORDER, ORDER), jnp.float32),
            dma,
            dma((2,)),
            dma((4,)),
            dma((ROUNDS, 2, LAYERS, 2)),
            dma((ROUNDS, SIDES)),
            dma((ROUNDS,)),
            dma((ROUNDS, 8)),
            dma((CHUNKS + 1,)),
            dma((2, 2)),
            dma((CHUNKS,)),
            dma((2,)),
            dma((ROUNDS, 2, 2)),
            dma((ROUNDS,)),
            dma((ROUNDS, 2, 4)),
            dma((3,)),
            dma((CHUNKS,)),
            dma((ROUNDS, 2, LAYERS, 2)),
            dma((ROUNDS, 2, LAYERS)),
            dma((ROUNDS, 2, LAYERS, 2)),
            dma((CHUNKS + 1,)),
            dma((2, CHUNKS)),
            dma((2,)),
            dma((2,)),
            dma((CHUNKS,)),
        ],
        compiler_params=pltpu.CompilerParams(
            collective_id=0, has_side_effects=True, vmem_limit_bytes=48 * 2**20
        ),
        cost_estimate=pl.CostEstimate(
            flops=12 * ORDER * PAIR * PAIR, bytes_accessed=3 * 2**20, transcendentals=0
        ),
    )(covariance, turn)


def solution(mesh):
    placed = (P("row", "col"), P(None, "col", "row", None), P())
    return jax.shard_map(
        per_device, mesh=mesh, in_specs=placed, out_specs=P("row", "col"), check_vma=False
    )
```

time: 1100 us -> 180 us (0.16)
  the two profiles are of different devices: /device:TPU:2 before, /device:TPU:12 now
where the time goes in v2:
time: 180 us; the launch traced here: 179 us
  Pallas kernels  175 us (97%)
  local copies, waits for them, and re-layouts  3.21 us (2%)
    pallas_call x1, Pallas kernels, per_device(): pl.pallas_call(kernel, out_shape=jax.ShapeDtypeStruct((ORDER, PAIR), jnp....  175 us

profile of v2, /device:TPU:12, one launch (start us, length us, event | category | flops | bytes accessed | tf_op | source)
XLA Modules:
  0.0 179.3 jit_solution(17069138679800696307)
XLA Ops:
  0.0 0.9 compare_reduce_fusion
  0.9 0.9 slice_bitcast_fusion.1
  1.8 0.1 reverse_select_fusion.turn
  1.9 0.0 copy-start
  1.9 1.3 copy-done
  3.2 175.1 %shard_map.37 = f32[384,768]{1,0:T(8,128)S(1)} custom-call(f32[384,768]{1,0:T(8,128)S(1)} %copy-done, f32[2,2,24,384]{3,2,1,0:T(8,128)S(1)} %reverse_select_fusion.turn), custom_call_target="tpu_custom_call" | custom-call | flops 2717908992 | bytes 3145728 | tf_op jit(solution)/shard_map/pallas_call | solution.py:557
  178.3 1.0 copy.6
  (1 shorter events, 0.0 us)
Async XLA Ops:
  1.9 1.3 copy-start

commit v3 on v2

--- a/solution.py
+++ b/solution.py
@@ -64,10 +64,10 @@
         return (device[0] == row) & (device[1] == col)
 
     def left_target(half, reach):
-        return (2 * col + layer % 2, 4 * (layer // 2) + 2 * reach + half)
+        return (2 * col + layer % 2, 4 * side + 2 * reach + half)
 
     def left_source(index):
-        return (SIDES * (2 * along + parity) + index, pair)
+        return (SIDES * (2 * index + parity) + along, pair)
 
     def peer(step):
         return (row, (col + 4 * step) % 16)
@@ -171,10 +171,13 @@
     def left_piece(index, half):
         return turn.at[index, half]
 
+    def left_piece_slot(index):
+        return left.at[index, side, layer % 2, layer // 2]
+
     def left_copy(index, half, reach):
         return remote(
-            left_piece(index, half), left.at[index, layer, side], left_out.at[index, half, reach],
-            left_sem.at[index, side], left_target(half, reach),
+            left_piece(index, half), left_piece_slot(index), left_out.at[index, half, reach],
+            left_sem.at[index, layer // 2], left_target(half, reach),
         )
 
     def left_start(index):
@@ -183,44 +186,49 @@
                 here = same(left_target(half, reach))
                 pl.when(here)(
                     pltpu.make_async_copy(
-                        left_piece(index, half), left.at[index, layer, side],
-                        left_sem.at[index, side],
+                        left_piece(index, half), left_piece_slot(index),
+                        left_sem.at[index, layer // 2],
                     ).start
                 )
                 pl.when(jnp.logical_not(here))(left_copy(index, half, reach).start)
 
-    group = 2 * along + parity
-
-    def mirror_copy(index):
-        slot = left.at[index, group]
-        return remote(slot, slot, mirror_out.at[index], mirror_sem.at[index], partner)
-
-    def spread_copy(index, which, step):
-        number = 2 * along + (parity if which == 0 else 1 - parity)
-        slot = left.at[index, number]
-        return remote(
-            slot, slot, spread_out.at[index, which, step], spread_sem.at[index, number], peer(step)
-        )
-
-    def left_mirror(index):
-        for number in range(SIDES):
-            arrived(left.at[index, group, number], left_sem.at[index, number])
-        mirror_copy(index).start()
+    def mirror_copy(index, number):
+        slot = left.at[index, along, parity, number]
+        return remote(
+            slot, slot, mirror_out.at[index, number], mirror_sem.at[index, number], partner
+        )
+
+    def spread_copy(index, which, number, step):
+        half = parity if which == 0 else 1 - parity
+        slot, sem = left.at[index, along, half, number], spread_sem.at[index, along, half]
+        return remote(slot, slot, spread_out.at[index, which, number, step], sem, peer(step))
+
+    def left_pass(index, number):
+        arrived(left.at[index, along, parity, number], left_sem.at[index, number])
+        mirror_copy(index, number).start()
         for step in range(1, 4):
-            spread_copy(index, 0, step).start()
-
-    def left_spread(index):
-        arrived(left.at[index, 2 * along + 1 - parity], mirror_sem.at[index])
+            spread_copy(index, 0, number, step).start()
+
+    def left_relay(index, number):
+        arrived(left.at[index, along, 1 - parity, number], mirror_sem.at[index, number])
         for step in range(1, 4):
-            spread_copy(index, 1, step).start()
+            spread_copy(index, 1, number, step).start()
+
+    def left_hooks(index, step):
+        pl.when((step >= 1) & (step < 5))(lambda: left_pass(index, step - 1))
+        pl.when(step >= 3)(lambda: left_relay(index, step - 3))
 
     def left_finish(index):
         for step in range(1, 4):
             for which in range(2):
-                number = 2 * ((along + step) % 4) + which
-                arrived(left.at[index, number], spread_sem.at[index, number])
+                number = (along + step) % 4
+                arrived(left.at[index, number, which], spread_sem.at[index, number, which])
         for half in range(2):
-            part = left[index, 4 * half:4 * half + 4].reshape(ORDER, ORDER)
+            pieces = [
+                left[index, y, z % 2, z // 2]
+                for z in range(4 * half, 4 * half + 4) for y in range(SIDES)
+            ]
+            part = jnp.concatenate(pieces, 0)
             left_high[index, half], left_low[index, half] = split(part.T)
 
     def slot_of(index, half, number, which):
@@ -335,23 +343,26 @@
     def _():
         for half in halves:
             pair_copy(half).start()
+        to_diagonal.start()
+
+    @pl.when(is_main)
+    def _():
+        to_mate.start()
+        for half in halves:
+            own_piece(half).start()
 
     left_start(0)
 
     @pl.when(is_helper)
     def _():
-        for number in range(CHUNKS):
-            both_copy(number).start()
-        to_diagonal.start()
         arrived(piece_slot(1, 0, parity), pair_sem.at[2])
         arrived(piece_slot(1, 0, 1 - parity), pair_sem.at[3])
         chain_send(1, 0)
+        for number in range(CHUNKS):
+            both_copy(number).start()
 
     @pl.when(is_main)
     def _():
-        to_mate.start()
-        for half in halves:
-            own_piece(half).start()
         for half in halves:
             own_piece(half).wait()
             arrived(piece_slot(0, half, 1 - parity), pair_sem.at[half])
@@ -369,8 +380,7 @@
                 chain_step(0, half, step)
 
         pl.when(is_helper)(lambda: chain_step(1, 0, step))
-        pl.when(step == 2)(lambda: left_mirror(0))
-        pl.when(step == 4)(lambda: left_spread(0))
+        left_hooks(0, step)
 
         @pl.when(is_main & (step >= 3))
         def _():
@@ -378,8 +388,8 @@
             arrived(chunk(both, 1 - parity, number), both_sem.at[number])
             mate_both(number).start()
 
+
     left_start(1)
-
     left_finish(0)
 
     def left_of(index, half):
@@ -445,11 +455,14 @@
     @pl.when(relays)
     def _():
         for number in range(CHUNKS):
-            arrived(passing.at[pl.ds(number * CHUNK, CHUNK)], passing_sem.at[number])
+            rows = pl.ds(number * CHUNK, CHUNK)
+            arrived(passing.at[rows], passing_sem.at[number])
             passing_copy(number).start()
 
-    left_mirror(1)
-    left_spread(1)
+    @pl.loop(0, LAYERS - 1)
+    def _(step):
+        left_hooks(1, step)
+
     chain_finish(1, 0)
     left_finish(1)
 
@@ -497,10 +510,14 @@
             for reach in range(2):
                 device = left_target(half, reach)
                 pl.when(jnp.logical_not(same(device)))(left_copy(index, half, reach).wait_send)
-        mirror_copy(index).wait_send()
-        for step in range(1, 4):
-            spread_copy(index, 0, step).wait_send()
-            spread_copy(index, 1, step).wait_send()
+
+        @pl.loop(0, 4)
+        def _(number):
+            mirror_copy(index, number).wait_send()
+            for step in range(1, 4):
+                spread_copy(index, 0, number, step).wait_send()
+                spread_copy(index, 1, number, step).wait_send()
+
     for half in range(2):
         through = uses_relay & (half == far_half)
         plain = jnp.logical_not(same(block_target(half))) & jnp.logical_not(through)
@@ -561,7 +578,7 @@
         out_specs=pl.BlockSpec(memory_space=pltpu.VMEM),
         scratch_shapes=[
             pltpu.VMEM((ROUNDS, 2, LAYERS, 2, 2 * PIECE, ORDER), jnp.float32),
-            pltpu.VMEM((ROUNDS, LAYERS, SIDES, PIECE, ORDER), jnp.float32),
+            pltpu.VMEM((ROUNDS, SIDES, 2, 4, PIECE, ORDER), jnp.float32),
             pltpu.VMEM((2, ORDER, PAIR), jnp.float32),
             pltpu.VMEM((2, 2, ORDER, ORDER), jnp.float32),
             pltpu.VMEM((2, ORDER, ORDER), jnp.float32),
@@ -575,16 +592,16 @@
             dma((2,)),
             dma((4,)),
             dma((ROUNDS, 2, LAYERS, 2)),
-            dma((ROUNDS, SIDES)),
-            dma((ROUNDS,)),
-            dma((ROUNDS, 8)),
+            dma((ROUNDS, 4)),
+            dma((ROUNDS, 4)),
+            dma((ROUNDS, SIDES, 2)),
             dma((CHUNKS + 1,)),
             dma((2, 2)),
             dma((CHUNKS,)),
             dma((2,)),
             dma((ROUNDS, 2, 2)),
-            dma((ROUNDS,)),
-            dma((ROUNDS, 2, 4)),
+            dma((ROUNDS, 4)),
+            dma((ROUNDS, 2, 4, 4)),
             dma((3,)),
             dma((CHUNKS,)),
             dma((ROUNDS, 2, LAYERS, 2)),

time: 180 us -> 173 us (0.961)
  the two profiles are of different devices: /device:TPU:12 before, /device:TPU:193 now
where the time goes in v3:
time: 173 us; the launch traced here: 172 us
  Pallas kernels  168 us (97%)
  local copies, waits for them, and re-layouts  3.21 us (2%)
    pallas_call x1, Pallas kernels, per_device(): pl.pallas_call(kernel, out_shape=jax.ShapeDtypeStruct((ORDER, PAIR), jnp....  168 us

profile of v3, /device:TPU:193, one launch (start us, length us, event | category | flops | bytes accessed | tf_op | source)
XLA Modules:
  0.0 172.4 jit_solution(14180964446765381824)
XLA Ops:
  0.0 0.9 compare_reduce_fusion
  0.9 0.9 slice_bitcast_fusion.1
  1.8 0.1 reverse_select_fusion.turn
  1.9 0.0 copy-start
  1.9 1.3 copy-done
  3.2 168.2 %shard_map.37 = f32[384,768]{1,0:T(8,128)S(1)} custom-call(f32[384,768]{1,0:T(8,128)S(1)} %copy-done, f32[2,2,24,384]{3,2,1,0:T(8,128)S(1)} %reverse_select_fusion.turn), custom_call_target="tpu_custom_call" | custom-call | flops 2717908992 | bytes 3145728 | tf_op jit(solution)/shard_map/pallas_call | solution.py:574
  171.4 1.0 copy.6
  (1 shorter events, 0.0 us)
Async XLA Ops:
  1.9 1.3 copy-start

commit v4 on v3

--- a/solution.py
+++ b/solution.py
@@ -381,6 +381,7 @@
 
         pl.when(is_helper)(lambda: chain_step(1, 0, step))
         left_hooks(0, step)
+        pl.when(step == 4)(lambda: left_start(1))
 
         @pl.when(is_main & (step >= 3))
         def _():
@@ -389,7 +390,6 @@
             mate_both(number).start()
 
 
-    left_start(1)
     left_finish(0)
 
     def left_of(index, half):

time: 173 us -> 178 us (1.029)
  the two profiles are of different devices: /device:TPU:193 before, /device:TPU:56 now
where the time goes in v4:
time: 178 us; the launch traced here: 177 us
  Pallas kernels  173 us (97%)
  local copies, waits for them, and re-layouts  3.21 us (2%)
    pallas_call x1, Pallas kernels, per_device(): pl.pallas_call(kernel, out_shape=jax.ShapeDtypeStruct((ORDER, PAIR), jnp....  173 us

profile of v4, /device:TPU:56, one launch (start us, length us, event | category | flops | bytes accessed | tf_op | source)
XLA Modules:
  0.0 177.4 jit_solution(16537206167212019230)
XLA Ops:
  0.0 0.9 compare_reduce_fusion
  0.9 0.9 slice_bitcast_fusion.1
  1.8 0.1 reverse_select_fusion.turn
  1.9 0.0 copy-start
  1.9 1.3 copy-done
  3.2 173.2 %shard_map.37 = f32[384,768]{1,0:T(8,128)S(1)} custom-call(f32[384,768]{1,0:T(8,128)S(1)} %copy-done, f32[2,2,24,384]{3,2,1,0:T(8,128)S(1)} %reverse_select_fusion.turn), custom_call_target="tpu_custom_call" | custom-call | flops 2717908992 | bytes 3145728 | tf_op jit(solution)/shard_map/pallas_call | solution.py:574
  176.4 1.0 copy.6
  (1 shorter events, 0.0 us)
Async XLA Ops:
  1.9 1.3 copy-start

commit v5 on v3

--- a/solution.py
+++ b/solution.py
@@ -473,16 +473,20 @@
         ref = fresh.at[core, slot]
         return remote(ref, ref, mate_fresh_out.at[slot], fresh_sem.at[core, slot], mate)
 
-    @pl.loop(0, 2)
-    def _(step):
-        slot = jnp.where(step == 0, 1 - far_slot, far_slot)
+    def rows_of(number, slot):
+        return right[1, number, pl.ds(4 * slot, 4)].reshape(ORDER, ORDER)
+
+    def second_left(slot):
         arrive_fresh(core, slot)
         mate_fresh(slot).start()
+        total = product(left_of(1, core), split(fresh[core, slot]))
         arrive_fresh(1 - core, slot)
-        total = product(left_of(1, 0), split(fresh[0, slot]))
-        total += product(left_of(1, 1), split(fresh[1, slot]))
-        columns = pl.ds(pl.multiple_of(slot * ORDER, 128), ORDER)
-        mid_high[:, columns], mid_low[:, columns] = split(total)
+        return split(total + product(left_of(1, 1 - core), split(fresh[1 - core, slot])))
+
+    near = second_left(1 - far_slot)
+    for number in range(2):
+        stage[:, pl.ds(number * ORDER, ORDER)] = product(near, split(rows_of(number, 1 - far_slot)))
+    mid_high[:, :ORDER], mid_low[:, :ORDER] = second_left(far_slot)
 
     def final_copy(number):
         columns = pl.ds(number * ORDER, ORDER)
@@ -493,8 +497,8 @@
 
     for number in range(2):
         columns = pl.ds(number * ORDER, ORDER)
-        turned = right[1, number].reshape(PAIR, ORDER)
-        value = product((mid_high[...], mid_low[...]), split(turned))
+        ahead = (mid_high[:, :ORDER], mid_low[:, :ORDER])
+        value = stage[:, columns] + product(ahead, split(rows_of(number, far_slot)))
 
         @pl.when(is_main)
         def _():

time: 173 us -> 172 us (level)
  no operation moved by 1% of the time
where the time goes in v5:
time: 172 us
  Pallas kernels  168 us (98%)
  local copies, waits for them, and re-layouts  3.21 us (2%)
    pallas_call x1, Pallas kernels, per_device(): pl.pallas_call(kernel, out_shape=jax.ShapeDtypeStruct((ORDER, PAIR), jnp....  168 us

profile of v5, /device:TPU:193, one launch (start us, length us, event | category | flops | bytes accessed | tf_op | source)
XLA Modules:
  0.0 172.2 jit_solution(5408508730127327064)
XLA Ops:
  0.0 0.9 compare_reduce_fusion
  0.9 0.9 slice_bitcast_fusion.1
  1.8 0.1 reverse_select_fusion.turn
  1.9 0.0 copy-start
  1.9 1.3 copy-done
  3.2 168.0 %shard_map.37 = f32[384,768]{1,0:T(8,128)S(1)} custom-call(f32[384,768]{1,0:T(8,128)S(1)} %copy-done, f32[2,2,24,384]{3,2,1,0:T(8,128)S(1)} %reverse_select_fusion.turn), custom_call_target="tpu_custom_call" | custom-call | flops 2717908992 | bytes 3145728 | tf_op jit(solution)/shard_map/pallas_call | solution.py:578
  171.1 1.0 copy.6
  (1 shorter events, 0.0 us)
Async XLA Ops:
  1.9 1.3 copy-start
